TPU v7x, 32 devices: a whole 2x2x4 slice. The times are simulated.
32 devices in a mesh: dp: 4 (over y, core), expert: 8 (over z, x).
Axes of the slice: x: 2, y: 2, z: 4, core: 2. Of those that a mesh axis runs over, the one named last changes fastest.
Arguments:
- x_in: bfloat16 [4096, 1024], P(('dp', 'expert')), may hold values from -6 to 6
- grad_out: bfloat16 [4096, 1024], P(('dp', 'expert')), may hold values from -6 to 6
- routes: int32 [4096, 8], P(('dp', 'expert')), may hold values from 0 to 7, as said below
- gate_probs: float32 [4096, 8], P(('dp', 'expert')), may hold values from 0.05 to 1
- gate_up: bfloat16 [8, 1024, 768], P('expert'), may hold values from -0.1875 to 0.1875
- down: bfloat16 [8, 1024, 384], P('expert'), may hold values from -0.3125 to 0.3125
Outputs:
- grad_in: bfloat16 [4096, 1024], P(('dp', 'expert'))
- grad_gate_up: float32 [8, 1024, 768], P('expert', 'dp')
- grad_down: float32 [8, 1024, 384], P('expert', 'dp')
Inputs may be any that keep to these rules, and one draw needn't show every extreme that they name: `routes`: each row names 8 different experts. Among the rows of one device no expert is named more than 128 times, and on every device some expert is named exactly 128 times.
All inputs are finite; a program needn't handle non-finite values.
Results may differ from a plain program's by a relative error of at most 0.02.
Values may be sent and summed in bfloat16 or wider, within the bound.
A program may use at most 64 MiB of HBM per device.

v0:
```python
import jax
import jax.numpy as jnp
from jax import lax
from jax.sharding import PartitionSpec as P


def slot_ranks(flat_ids, experts):
    onehot = (flat_ids[:, None] == jnp.arange(experts, dtype=jnp.int32)[None, :]).astype(jnp.int32)
    before = jnp.cumsum(onehot, axis=0) - onehot
    return jnp.sum(before * onehot, axis=1)


def dispatch_table(route_block, experts, capacity):
    flat_ids = route_block.reshape(-1)
    count_rows = flat_ids.shape[0]
    slot_rank = slot_ranks(flat_ids, experts)
    entry_pos = flat_ids * capacity + slot_rank
    slot_table = jnp.full((experts * capacity,), count_rows, jnp.int32)
    slot_table = slot_table.at[entry_pos].set(jnp.arange(count_rows, dtype=jnp.int32))
    return (slot_table, entry_pos)


def send_rows(x_block, grad_block, prob_block, slot_table, top_count):
    width = x_block.shape[1]
    token_pos = slot_table // top_count
    x_padded = jnp.concatenate([x_block, jnp.zeros((1, width), jnp.bfloat16)], 0)
    grad_padded = jnp.concatenate([grad_block, jnp.zeros((1, width), jnp.bfloat16)], 0)
    prob_padded = jnp.concatenate([prob_block.reshape(-1), jnp.zeros((1,), jnp.float32)], 0)
    sent_rows = x_padded[token_pos]
    sent_grads = (
        prob_padded[slot_table][:, None] * grad_padded[token_pos].astype(jnp.float32)
    ).astype(jnp.bfloat16)
    return (sent_rows, sent_grads)


def expert_rows(rows_in, scaled, proj_weight, down_weight):
    hidden_units = down_weight.shape[1]
    projected = jnp.dot(rows_in, proj_weight, preferred_element_type=jnp.float32)
    gate_pre = projected[:, :hidden_units]
    up_part = projected[:, hidden_units:]
    sigmoid_v = jax.nn.sigmoid(gate_pre)
    activated = gate_pre * sigmoid_v
    hidden = (activated * up_part).astype(jnp.bfloat16)
    grad_hidden = jnp.dot(scaled, down_weight, preferred_element_type=jnp.float32)
    grad_gate = grad_hidden * up_part * sigmoid_v * (1.0 + gate_pre * (1.0 - sigmoid_v))
    grad_proj = jnp.concatenate([grad_gate, grad_hidden * activated], 1).astype(jnp.bfloat16)
    grad_rows = lax.dot_general(
        grad_proj, proj_weight, (((1,), (1,)), ((), ())), preferred_element_type=jnp.float32
    ).astype(jnp.bfloat16)
    return (grad_rows, grad_proj, hidden)


def weight_terms(rows_in, scaled, grad_proj, hidden):
    first = lax.dot_general(
        rows_in, grad_proj, (((0,), (0,)), ((), ())), preferred_element_type=jnp.float32
    )
    second = lax.dot_general(
        scaled, hidden, (((0,), (0,)), ((), ())), preferred_element_type=jnp.float32
    )
    return jnp.concatenate([first, second], 1)


def per_device(x_in, grad_out, routes, gate_probs, gate_up, down):
    owners = lax.axis_size("expert")
    tokens_here = x_in.shape[0]
    top_count = routes.shape[1]
    width = x_in.shape[1]
    capacity = min(tokens_here, tokens_here * top_count * 9 // (8 * owners))
    slot_table, entry_pos = dispatch_table(routes, owners, capacity)
    sent_rows, sent_grads = send_rows(x_in, grad_out, gate_probs, slot_table, top_count)
    sent_rows = sent_rows.reshape(owners, capacity, width)
    sent_grads = sent_grads.reshape(owners, capacity, width)
    proj_weight = gate_up[0]
    down_weight = down[0]
    recv_rows, recv_grads = (
        lax.all_to_all(sent_rows, "expert", split_axis=0, concat_axis=0, tiled=True),
        lax.all_to_all(sent_grads, "expert", split_axis=0, concat_axis=0, tiled=True),
    )
    rows_in = recv_rows.reshape(-1, width)
    scaled = recv_grads.reshape(-1, width)
    grad_rows, grad_proj, hidden = expert_rows(rows_in, scaled, proj_weight, down_weight)
    returned = lax.all_to_all(
        grad_rows.reshape(owners, capacity, width),
        "expert",
        split_axis=0,
        concat_axis=0,
        tiled=True,
    )
    hidden_units = hidden.shape[1]
    grad_term = weight_terms(rows_in, scaled, grad_proj, hidden)
    grad_share = lax.psum_scatter(
        grad_term.astype(jnp.bfloat16), "dp", scatter_dimension=0, tiled=True
    ).astype(jnp.float32)
    grad_gate_up = grad_share[None, :, : 2 * hidden_units]
    grad_down = grad_share[None, :, 2 * hidden_units :]
    entries = returned.reshape(-1, width)[entry_pos]
    grad_in = jnp.sum(
        entries.reshape(tokens_here, top_count, width).astype(jnp.float32), axis=1
    ).astype(jnp.bfloat16)
    return (grad_in, grad_gate_up, grad_down)


def solution(mesh):
    placed = (
        P(("dp", "expert"), None),
        P(("dp", "expert"), None),
        P(("dp", "expert"), None),
        P(("dp", "expert"), None),
        P("expert", None, None),
        P("expert", None, None),
    )
    return jax.shard_map(
        per_device,
        mesh=mesh,
        in_specs=placed,
        out_specs=(P(("dp", "expert"), None), P("expert", "dp", None), P("expert", "dp", None)),
        check_vma=False,
    )
```

profile of v0, /device:TPU:0, one launch (start us, length us, event | category | flops | bytes accessed | tf_op | source)
XLA Modules:
  0.0 221.7 jit_solution(3884974330897946986)
XLA Ops:
  7.2 0.8 broadcast_multiply_fusion
  8.0 0.8 copy.13
  9.0 0.1 copy.12
  9.1 0.1 mul.53
  9.2 2.3 %reduce-window.6 = s32[8,8,128]{2,1,0:T(8,128)S(1)} reduce-window(s32[8,8,128]{2,1,0:T(8,128)S(1)} %fusion.11, s32[]{:T(128)} %constant.29.clone.1), window={size=1x1x128 pad=0_0x0_0x127_0}, to_apply=%region_0.0 | reduce-window | flops 1040384 | bytes 65540 | tf_op jit(solution)/shard_map/reduce-window
  11.4 0.3 slice_reduce_fusion
  11.7 0.2 reduce-window.9
  12.0 4.3 %scatter_custom_fusion = s32[1024]{0:T(1024)S(1)} fusion(s32[1024]{0:T(1024)S(1)} %bitcast.54, s32[1024]{0:T(1024)S(1)} %iota.11, s32[]{:T(128)} %constant.14.clone.1), kind=kCustom, calls=%fused_computation.49 | custom fusion | bytes 4100 | tf_op jit(solution)/shard_map/scatter | solution.py:19
  16.4 1.0 concatenate.19
  17.3 5.4 %gather_fusion.2 = bf16[1024,1024]{1,0:T(8,128)(2,1)} fusion(bf16[129,1024]{1,0:T(8,128)(2,1)S(1)} %concatenate.19, s32[1024]{0:T(1024)S(1)} %get-tuple-element.12), kind=kCustom, calls=%fused_computation.2 | custom fusion | bytes 4198400 | tf_op jit(solution)/shard_map/gather | solution.py:29
  22.7 7.4 %all-to-all-start.1 = ((bf16[8,128,1024]{2,1,0:T(8,128)(2,1)}), bf16[8,128,1024]{2,1,0:T(8,128)(2,1)}, u32[]{:S(2)}, u32[]{:S(2)}) async-start(bf16[8,128,1024]{2,1,0:T(8,128)(2,1)} %bitcast.51), calls=%async_computation.1 | async-start | bytes 4194304 | tf_op jit(solution)/shard_map/all_to_all | solution.py:76
  30.1 0.1 copy.11
  30.3 5.4 %gather_fusion.1 = bf16[1024,1024]{1,0:T(8,128)(2,1)} fusion(bf16[129,1024]{1,0:T(8,128)(2,1)S(1)} %concatenate.18, s32[1024]{0:T(1024)S(1)} %get-tuple-element.12), kind=kCustom, calls=%fused_computation.1 | custom fusion | bytes 4198400 | tf_op jit(solution)/shard_map/gather | solution.py:31
  35.7 6.1 %gather_fusion = f32[1024]{0:T(1024)S(1)} fusion(f32[1025]{0:T(1024)S(1)} %pad_maximum_fusion.4, s32[1024]{0:T(1024)S(1)} %get-tuple-element.11), kind=kCustom, calls=%fused_computation | custom fusion | bytes 12288 | tf_op jit(solution)/shard_map/gather | solution.py:31
  41.9 3.4 %fusion = bf16[8,128,1024]{2,1,0:T(8,128)(2,1)} fusion(bf16[8,128,1024]{2,1,0:T(8,128)(2,1)} %bitcast.50, f32[8,128]{1,0:T(8,128)S(1)} %bitcast.57), kind=kLoop, calls=%fused_computation.6 | loop fusion | flops 3145728 | bytes 4198400 | tf_op jit(solution)/shard_map/convert_element_type | solution.py:32
  45.2 33.2 %all-to-all-done.1 = bf16[8,128,1024]{2,1,0:T(8,128)(2,1)} async-done(((bf16[8,128,1024]{2,1,0:T(8,128)(2,1)}), bf16[8,128,1024]{2,1,0:T(8,128)(2,1)}, u32[]{:S(2)}, u32[]{:S(2)}) %all-to-all-start.1) | async-done | bytes 2097184 | tf_op jit(solution)/shard_map/all_to_all | solution.py:76
  78.4 4.3 %all-to-all-start = ((bf16[8,128,1024]{2,1,0:T(8,128)(2,1)}), bf16[8,128,1024]{2,1,0:T(8,128)(2,1)}, u32[]{:S(2)}, u32[]{:S(2)}) async-start(bf16[8,128,1024]{2,1,0:T(8,128)(2,1)} %fusion), calls=%async_computation | async-start | bytes 4194304 | tf_op jit(solution)/shard_map/all_to_all | solution.py:77
  82.9 5.1 %fusion.2 = f32[1024,768]{0,1:T(8,128)} fusion(bf16[1024,1024]{1,0:T(8,128)(2,1)} %bitcast.8, bf16[1,1024,768]{2,1,0:T(8,128)(2,1)S(1)} %copy-done), kind=kOutput, calls=%fused_computation.13 | convolution fusion | flops 1610612736 | bytes 6815744 | tf_op jit(solution)/shard_map/dot_general | solution.py:38
  88.0 42.7 %all-to-all-done = bf16[8,128,1024]{2,1,0:T(8,128)(2,1)} async-done(((bf16[8,128,1024]{2,1,0:T(8,128)(2,1)}), bf16[8,128,1024]{2,1,0:T(8,128)(2,1)}, u32[]{:S(2)}, u32[]{:S(2)}) %all-to-all-start) | async-done | bytes 2097184 | tf_op jit(solution)/shard_map/all_to_all | solution.py:77
  130.6 3.7 %convolution_convert_fusion.2 = bf16[1024,384]{0,1:T(8,128)(2,1)S(1)} fusion(bf16[1024,1024]{1,0:T(8,128)(2,1)} %bitcast.5, f32[1024,768]{0,1:T(8,128)} %fusion.2), kind=kOutput, calls=%fused_computation.20 | convolution fusion | flops 808058880 | bytes 6029312 | tf_op jit(solution)/shard_map/dot_general | solution.py:57
  134.3 3.1 %multiply_convert_fusion.2 = (bf16[1024,384]{0,1:T(8,128)(2,1)S(1)}, bf16[1024,384]{0,1:T(8,128)(2,1)S(1)}) fusion(f32[1024,768]{0,1:T(8,128)S(1)} %copy-done.4, bf16[1024,1024]{1,0:T(8,128)(2,1)} %bitcast.5, bf16[1,1024,384]{2,1,0:T(8,128)(2,1)S(1)} %copy-done.3), kind=kOutput, calls=%fused_computation.17 | convolution fusion | flops 810418176 | bytes 7602176 | tf_op jit(solution)/shard_map/dot_general | solution.py:44
  137.4 0.9 copy-done.5
  138.3 3.4 %convolution_convert_fusion.1 = bf16[1024,768]{0,1:T(8,128)(2,1)S(1)} fusion(bf16[1024,1024]{1,0:T(8,128)(2,1)} %bitcast.8, bf16[1024,384]{0,1:T(8,128)(2,1)S(1)} %get-tuple-element.10, bf16[1024,384]{0,1:T(8,128)(2,1)S(1)} %get-tuple-element.9), kind=kOutput, calls=%fused_computation.10 | convolution fusion | flops 1614544896 | bytes 5242880 | tf_op jit(solution)/shard_map/dot_general | solution.py:54
  141.7 1.6 pad_maximum_fusion
  143.4 4.3 %convolution_convert_fusion = bf16[1024,1024]{1,0:T(8,128)(2,1)} fusion(bf16[1,1024,768]{2,1,0:T(8,128)(2,1)S(1)} %copy-done, bf16[1024,384]{0,1:T(8,128)(2,1)} %copy-done.5, bf16[1024,384]{0,1:T(8,128)(2,1)S(1)} %get-tuple-element.9), kind=kOutput, calls=%fused_computation.9 | convolution fusion | flops 1614807040 | bytes 5242880 | tf_op jit(solution)/shard_map/dot_general | solution.py:47
  147.7 4.6 %all-to-all-start.2 = ((bf16[8,128,1024]{2,1,0:T(8,128)(2,1)}), bf16[8,128,1024]{2,1,0:T(8,128)(2,1)}, u32[]{:S(2)}, u32[]{:S(2)}) async-start(bf16[8,128,1024]{2,1,0:T(8,128)(2,1)} %bitcast.52), calls=%async_computation.2 | async-start | bytes 4194304 | tf_op jit(solution)/shard_map/all_to_all | solution.py:82
  152.3 47.6 %all-to-all-done.2 = bf16[8,128,1024]{2,1,0:T(8,128)(2,1)} async-done(((bf16[8,128,1024]{2,1,0:T(8,128)(2,1)}), bf16[8,128,1024]{2,1,0:T(8,128)(2,1)}, u32[]{:S(2)}, u32[]{:S(2)}) %all-to-all-start.2) | async-done | bytes 2097184 | tf_op jit(solution)/shard_map/all_to_all | solution.py:82
  199.9 7.9 %gather_fusion.3 = bf16[1024,1024]{1,0:T(8,128)(2,1)} fusion(bf16[1024,1024]{1,0:T(8,128)(2,1)} %bitcast.11, s32[1024]{0:T(1024)S(1)} %broadcast_clamp_fusion), kind=kCustom, calls=%fused_computation.3 | custom fusion | bytes 4198400 | tf_op jit(solution)/shard_map/gather | solution.py:96
  207.8 3.7 %bitcast_reduce_fusion = bf16[128,1024]{1,0:T(8,128)(2,1)} fusion(bf16[1024,1024]{1,0:T(8,128)(2,1)} %gather_fusion.3), kind=kLoop, calls=%fused_computation.8 | loop fusion | flops 917504 | bytes 2359296 | tf_op jit(solution)/shard_map/reduce_sum | solution.py:97
  211.6 1.1 convert_element_type.38
  212.8 1.1 copy.15
  214.0 0.9 copy.16
  (28 shorter events, 0.6 us)
Async XLA Ops:
  7.2 75.7 %copy-start = (bf16[1,1024,768]{2,1,0:T(8,128)(2,1)S(1)}, bf16[1,1024,768]{2,1,0:T(8,128)(2,1)}, u32[]{:S(2)}) copy-start(bf16[1,1024,768]{2,1,0:T(8,128)(2,1)} %param.10) | copy-start | bytes 4718596
  22.7 7.4 %copy-start.2 = (f32[128,8]{0,1:T(8,128)S(1)}, f32[128,8]{0,1:T(8,128)}, u32[]{:S(2)}) copy-start(f32[128,8]{0,1:T(8,128)} %param.9) | copy-start | bytes 12292
  22.7 7.6 %copy-start.1 = (bf16[128,1024]{1,0:T(8,128)(2,1)S(1)}, bf16[128,1024]{1,0:T(8,128)(2,1)}, u32[]{:S(2)}) copy-start(bf16[128,1024]{1,0:T(8,128)(2,1)} %param.7) | copy-start | bytes 786436
  22.7 55.7 %all-to-all-start.1 = ((bf16[8,128,1024]{2,1,0:T(8,128)(2,1)}), bf16[8,128,1024]{2,1,0:T(8,128)(2,1)}, u32[]{:S(2)}, u32[]{:S(2)}) async-start(bf16[8,128,1024]{2,1,0:T(8,128)(2,1)} %bitcast.51), calls=%async_computation.1 | async-start | bytes 4194304 | tf_op jit(solution)/shard_map/all_to_all | solution.py:76
  78.4 52.2 %all-to-all-start = ((bf16[8,128,1024]{2,1,0:T(8,128)(2,1)}), bf16[8,128,1024]{2,1,0:T(8,128)(2,1)}, u32[]{:S(2)}, u32[]{:S(2)}) async-start(bf16[8,128,1024]{2,1,0:T(8,128)(2,1)} %fusion), calls=%async_computation | async-start | bytes 4194304 | tf_op jit(solution)/shard_map/all_to_all | solution.py:77
  82.8 128.8 %reduce-scatter.2.cloned.1.call-start = ((), (), s32[]{:S(2)}) async-start(), calls=%async_computation.4 | async-start | bytes 2949120 | tf_op jit(solution)/shard_map/reduce_scatter | solution.py:91
  130.6 3.7 %copy-start.3 = (bf16[1,1024,384]{2,1,0:T(8,128)(2,1)S(1)}, bf16[1,1024,384]{2,1,0:T(8,128)(2,1)}, u32[]{:S(2)}) copy-start(bf16[1,1024,384]{2,1,0:T(8,128)(2,1)} %param.11) | copy-start | bytes 2359300
  130.6 3.7 %copy-start.4 = (f32[1024,768]{0,1:T(8,128)S(1)}, f32[1024,768]{0,1:T(8,128)}, u32[]{:S(2)}) copy-start(f32[1024,768]{0,1:T(8,128)} %fusion.2) | copy-start | bytes 9437188
  137.4 0.9 copy-start.5
  147.7 52.2 %all-to-all-start.2 = ((bf16[8,128,1024]{2,1,0:T(8,128)(2,1)}), bf16[8,128,1024]{2,1,0:T(8,128)(2,1)}, u32[]{:S(2)}, u32[]{:S(2)}) async-start(bf16[8,128,1024]{2,1,0:T(8,128)(2,1)} %bitcast.52), calls=%async_computation.2 | async-start | bytes 4194304 | tf_op jit(solution)/shard_map/all_to_all | solution.py:82
Sparse Core Ops, SparseCore 0:
  143.5 32.1 reduce-scatter.1
where the time goes:
time: 222 us
  waiting for transfers between devices  124 us (56%)
  local copies, waits for them, and re-layouts  34.8 us (16%)
  matrix products  19.6 us (9%)
  starting transfers between devices  16.4 us (7%)
  between operations  14.2 us (6%)
  other arithmetic  13.2 us (6%)
    all_to_all x1, waiting for transfers between devices, per_device(): lax.all_to_all(grad_rows.reshape(owners, capacity, width), 'expert', spli...  47.6 us
    all_to_all x1, waiting for transfers between devices, per_device(): lax.all_to_all(sent_grads, 'expert', split_axis=0, concat_axis=0, tiled=T...  42.7 us
    all_to_all x1, waiting for transfers between devices, per_device(): lax.all_to_all(sent_rows, 'expert', split_axis=0, concat_axis=0, tiled=True)  33.2 us
    gather x1, local copies, waits for them, and re-layouts, per_device(): entries = returned.reshape(-1, width)[entry_pos]  7.91 us
    all_to_all x1, starting transfers between devices, per_device(): lax.all_to_all(sent_rows, 'expert', split_axis=0, concat_axis=0, tiled=True)  7.38 us
    gather x1, local copies, waits for them, and re-layouts, send_rows(): prob_padded[slot_table][:, None]  6.14 us
    gather x1, local copies, waits for them, and re-layouts, send_rows(): grad_padded[token_pos].astype(jnp.float32)  5.38 us
    gather x1, local copies, waits for them, and re-layouts, send_rows(): sent_rows = x_padded[token_pos]  5.36 us
  transfers between devices with their start and end apart: 4, of which 3 were waited for; matrix products, arithmetic and copies ran while one was open for 16% of the time, Pallas kernels for 0%

commit v1 on v0

--- a/solution.py
+++ b/solution.py
@@ -60,7 +60,36 @@
     return jnp.concatenate([first, second], 1)
 
 
+def dense_device(x_in, grad_out, routes, gate_probs, gate_up, down):
+    owners = lax.axis_size("expert")
+    me = lax.axis_index("expert")
+    width = x_in.shape[1]
+    ids = jnp.arange(owners, dtype=jnp.int32)
+    prob_by_expert = jnp.sum(
+        jnp.where(routes[:, :, None] == ids[None, None, :], gate_probs[:, :, None], 0.0), axis=1
+    )
+    all_probs = lax.all_gather(prob_by_expert, "expert", axis=0, tiled=True)
+    rows_in = lax.all_gather(x_in, "expert", axis=0, tiled=True)
+    all_grads = lax.all_gather(grad_out, "expert", axis=0, tiled=True)
+    mine = jnp.sum(jnp.where(ids[None, :] == me, all_probs, 0.0), axis=1)
+    scaled = (mine[:, None] * all_grads.astype(jnp.float32)).astype(jnp.bfloat16)
+    grad_rows, grad_proj, hidden = expert_rows(rows_in, scaled, gate_up[0], down[0])
+    grad_in = lax.psum_scatter(grad_rows, "expert", scatter_dimension=0, tiled=True)
+    hidden_units = hidden.shape[1]
+    grad_term = weight_terms(rows_in, scaled, grad_proj, hidden)
+    grad_share = lax.psum_scatter(
+        grad_term.astype(jnp.bfloat16), "dp", scatter_dimension=0, tiled=True
+    ).astype(jnp.float32)
+    return (
+        grad_in,
+        grad_share[None, :, : 2 * hidden_units],
+        grad_share[None, :, 2 * hidden_units :],
+    )
+
+
 def per_device(x_in, grad_out, routes, gate_probs, gate_up, down):
+    if lax.axis_size("expert") == routes.shape[1]:
+        return dense_device(x_in, grad_out, routes, gate_probs, gate_up, down)
     owners = lax.axis_size("expert")
     tokens_here = x_in.shape[0]
     top_count = routes.shape[1]

time: 222 us -> 233 us (1.050)
  waiting for transfers between devices: 124 us -> 163 us
  blocking collectives: 0 us -> 32.4 us
  local copies, waits for them, and re-layouts: 34.8 us -> 4.29 us
  starting transfers between devices: 16.4 us -> 0.16 us
  other arithmetic: 13.2 us -> 3.57 us
  matrix products: 19.6 us -> 15.5 us
    all_to_all x3 -> x0, waiting for transfers between devices: 124 us -> none  [the longest x1 47.6 us: per_device(): lax.all_to_all(grad_rows.reshape(owners, capacity, width), 'expert', spli...]
    reduce_scatter x1 -> x2, waiting for transfers between devices: 0.01 us -> 96.4 us  [the longest x1 69 us: dense_device(): lax.psum_scatter(grad_rows, 'expert', scatter_dimension=0, tiled=True)]
    all_gather x0 -> x2, waiting for transfers between devices: none -> 65.2 us  [the longest x1 44.9 us: dense_device(): all_grads = lax.all_gather(grad_out, 'expert', axis=0, tiled=True)]
    all_gather x0 -> x1, blocking collectives: none -> 32.4 us  [dense_device(): all_probs = lax.all_gather(prob_by_expert, 'expert', axis=0, tiled=True)]
    gather x4 -> x0, local copies, waits for them, and re-layouts: 24.8 us -> none  [the longest x1 7.91 us: per_device(): entries = returned.reshape(-1, width)[entry_pos]]
    all_to_all x3 -> x0, starting transfers between devices: 16.3 us -> none  [the longest x1 7.38 us: per_device(): lax.all_to_all(sent_rows, 'expert', split_axis=0, concat_axis=0, tiled=True)]
    scatter x1 -> x0, local copies, waits for them, and re-layouts: 4.31 us -> none  [dispatch_table(): slot_table.at[entry_pos].set(jnp.arange(count_rows, dtype=jnp.int32))]
    convert_element_type x3 -> x1, other arithmetic: 4.52 us -> 1.14 us  [dense_device(): grad_share = lax.psum_scatter(grad_term.astype(jnp.bfloat16), 'dp', scatt...]
  transfers between devices with their start and end apart: 4 -> 4, of which waited for: 3 -> 4; matrix products, arithmetic and copies ran while one was open for 16% -> 5% of each run, Pallas kernels for 0% -> 0%
where the time goes in v1:
time: 233 us
  waiting for transfers between devices  163 us (70%)
  blocking collectives  32.4 us (14%)
  matrix products  15.5 us (7%)
  between operations  13.9 us (6%)
  local copies, waits for them, and re-layouts  4.29 us (2%)
  other arithmetic  3.57 us (2%)
    reduce_scatter x1, waiting for transfers between devices, dense_device(): lax.psum_scatter(grad_rows, 'expert', scatter_dimension=0, tiled=True)  69 us
    all_gather x1, waiting for transfers between devices, dense_device(): all_grads = lax.all_gather(grad_out, 'expert', axis=0, tiled=True)  44.9 us
    all_gather x1, blocking collectives, dense_device(): all_probs = lax.all_gather(prob_by_expert, 'expert', axis=0, tiled=True)  32.4 us
    reduce_scatter x1, waiting for transfers between devices, dense_device(): lax.psum_scatter(grad_term.astype(jnp.bfloat16), 'dp', scatter_dimension=...  27.4 us
    all_gather x1, waiting for transfers between devices, dense_device(): rows_in = lax.all_gather(x_in, 'expert', axis=0, tiled=True)  20.4 us
    dot_general x1, matrix products, expert_rows(): jnp.dot(rows_in, proj_weight, preferred_element_type=jnp.float32)  5.07 us
  transfers between devices with their start and end apart: 4, of which 4 were waited for; matrix products, arithmetic and copies ran while one was open for 5% of the time, Pallas kernels for 0%

profile of v1, /device:TPU:0, one launch (start us, length us, event | category | flops | bytes accessed | tf_op | source)
XLA Modules:
  0.0 232.8 jit_solution(4899741934972506858)
XLA Ops:
  7.2 0.0 copy-start
  7.2 0.0 all-gather.5.cloned.1.call-start
  7.2 0.7 all-gather.5.cloned.1.call-update
  7.9 0.0 all-gather.3.cloned.1.call-start
  8.0 0.7 all-gather.3.cloned.1.call-update
  8.7 0.0 reduce-scatter.5.cloned.1.call-start
  8.7 0.7 select_reduce_fusion.1
  9.4 32.4 %all_gather.9 = f32[1024,8]{0,1:T(8,128)S(1)} all-gather(f32[128,8]{0,1:T(8,128)S(1)} %select_reduce_fusion.1), channel_id=1, replica_groups=mesh['dp'=4,'expert'=8] {'expert'}, dimensions={0}, use_global_device_ids=true | all-gather | bytes 36864 | tf_op jit(solution)/shard_map/all_gather | solution.py:71
  41.8 0.1 select_reduce_fusion
  41.9 20.4 %all-gather.5.cloned.1.call-done = bf16[1024,1024]{1,0:T(8,128)(2,1)} async-done(((bf16[128,1024]{1,0:T(8,128)(2,1)}), bf16[1024,1024]{1,0:T(8,128)(2,1)}) %all-gather.5.cloned.1.call-update) | async-done | bytes 2097168 | tf_op jit(solution)/shard_map/all_gather | solution.py:72
  62.3 0.0 copy-done
  62.3 5.1 %fusion.1 = f32[1024,768]{0,1:T(8,128)} fusion(bf16[1024,1024]{1,0:T(8,128)(2,1)} %all-gather.5.cloned.1.call-done, bf16[1,1024,768]{2,1,0:T(8,128)(2,1)S(1)} %copy-done), kind=kOutput, calls=%fused_computation.6 | convolution fusion | flops 1610612736 | bytes 6815744 | tf_op jit(solution)/shard_map/dot_general | solution.py:38
  67.4 44.9 %all-gather.3.cloned.1.call-done = bf16[1024,1024]{1,0:T(8,128)(2,1)} async-done(((bf16[128,1024]{1,0:T(8,128)(2,1)}), bf16[1024,1024]{1,0:T(8,128)(2,1)}) %all-gather.3.cloned.1.call-update) | async-done | bytes 2097168 | tf_op jit(solution)/shard_map/all_gather | solution.py:73
  112.3 3.9 %convolution_convert_fusion.2 = bf16[1024,384]{0,1:T(8,128)(2,1)S(1)} fusion(bf16[1024,1024]{1,0:T(8,128)(2,1)} %all-gather.3.cloned.1.call-done, f32[1024]{0:T(1024)S(1)} %select_reduce_fusion, f32[1024,768]{0,1:T(8,128)} %fusion.1), kind=kOutput, calls=%fused_computation.14 | convolution fusion | flops 811204608 | bytes 6033408 | tf_op jit(solution)/shard_map/dot_general | solution.py:57
  116.1 0.0 copy-done.3
  116.1 0.2 copy-done.4
  116.3 1.6 multiply_convert_fusion.3
  118.0 0.0 copy-start.5
  118.0 0.9 copy-done.5
  118.8 1.8 fusion.4
  120.7 1.6 pad_maximum_fusion
  122.3 0.0 reduce-scatter.5.cloned.1.call-update
  122.3 0.0 reduce-scatter.3.cloned.1.call-start
  122.4 1.1 copy-done.6
  123.4 3.2 %convolution_convert_fusion = bf16[1024,1024]{1,0:T(8,128)(2,1)} fusion(bf16[1,1024,768]{2,1,0:T(8,128)(2,1)S(1)} %copy-done, bf16[1024,384]{0,1:T(8,128)(2,1)S(1)} %copy-done.6, bf16[1024,384]{0,1:T(8,128)(2,1)S(1)} %get-tuple-element.9), kind=kOutput, calls=%fused_computation.2 | convolution fusion | flops 1614807040 | bytes 5242880 | tf_op jit(solution)/shard_map/dot_general | solution.py:47
  126.6 0.0 reduce-scatter.3.cloned.1.call-update
  126.6 27.4 %reduce-scatter.5.cloned.1.call-done = bf16[256,1152]{0,1:T(8,128)(2,1)} async-done(((bf16[1024,1152]{0,1:T(8,128)(2,1)}), bf16[256,1152]{0,1:T(8,128)(2,1)}) %reduce-scatter.5.cloned.1.call-update) | async-done | bytes 589840 | tf_op jit(solution)/shard_map/reduce_scatter | solution.py:80
  154.0 1.1 convert_element_type.21
  155.2 0.1 slice_bitcast_fusion
  155.3 1.1 copy.13
  156.4 0.9 copy.14
  157.3 69.0 %reduce-scatter.3.cloned.1.call-done = bf16[128,1024]{1,0:T(8,128)(2,1)} async-done(((bf16[1024,1024]{1,0:T(8,128)(2,1)}), bf16[128,1024]{1,0:T(8,128)(2,1)}) %reduce-scatter.3.cloned.1.call-update) | async-done | bytes 262160 | tf_op jit(solution)/shard_map/reduce_scatter | solution.py:77
  (9 shorter events, 0.0 us)
Async XLA Ops:
  7.2 55.1 %copy-start = (bf16[1,1024,768]{2,1,0:T(8,128)(2,1)S(1)}, bf16[1,1024,768]{2,1,0:T(8,128)(2,1)}, u32[]{:S(2)}) copy-start(bf16[1,1024,768]{2,1,0:T(8,128)(2,1)} %param.10) | copy-start | bytes 4718596
  7.2 55.1 %all-gather.5.cloned.1.call-start = ((), (), s32[]{:S(2)}) async-start(), calls=%async_computation.3 | async-start | bytes 2359296 | tf_op jit(solution)/shard_map/all_gather | solution.py:72
  7.9 104.3 %all-gather.3.cloned.1.call-start = ((), (), s32[]{:S(2)}) async-start(), calls=%async_computation.2 | async-start | bytes 2359296 | tf_op jit(solution)/shard_map/all_gather | solution.py:73
  8.7 145.4 %reduce-scatter.5.cloned.1.call-start = ((), (), s32[]{:S(2)}) async-start(), calls=%async_computation.5 | async-start | bytes 2949120 | tf_op jit(solution)/shard_map/reduce_scatter | solution.py:80
  67.4 48.7 %copy-start.3 = (bf16[1,1024,384]{2,1,0:T(8,128)(2,1)S(1)}, bf16[1,1024,384]{2,1,0:T(8,128)(2,1)}, u32[]{:S(2)}) copy-start(bf16[1,1024,384]{2,1,0:T(8,128)(2,1)} %param.11) | copy-start | bytes 2359300
  112.2 3.9 %copy-start.2 = (bf16[1024,1024]{1,0:T(8,128)(2,1)S(1)}, bf16[1024,1024]{1,0:T(8,128)(2,1)}, u32[]{:S(2)}) copy-start(bf16[1024,1024]{1,0:T(8,128)(2,1)} %all-gather.3.cloned.1.call-done) | copy-start | bytes 6291460
  112.2 4.1 %copy-start.4 = (f32[1024,768]{0,1:T(8,128)S(1)}, f32[1024,768]{0,1:T(8,128)}, u32[]{:S(2)}) copy-start(f32[1024,768]{0,1:T(8,128)} %fusion.1) | copy-start | bytes 9437188
  116.3 2.5 %copy-start.1 = (bf16[1024,1024]{1,0:T(8,128)(2,1)S(1)}, bf16[1024,1024]{1,0:T(8,128)(2,1)}, u32[]{:S(2)}) copy-start(bf16[1024,1024]{1,0:T(8,128)(2,1)} %all-gather.5.cloned.1.call-done) | copy-start | bytes 6291460
  118.0 0.9 copy-start.5
  122.3 1.1 copy-start.6
  122.3 104.0 %reduce-scatter.3.cloned.1.call-start = ((), (), s32[]{:S(2)}) async-start(), calls=%async_computation.4 | async-start | bytes 2359296 | tf_op jit(solution)/shard_map/reduce_scatter | solution.py:77
Sparse Core Ops, SparseCore 0:
  10.1 52.1 all-gather.4
  64.4 47.7 all-gather.2
  122.4 31.5 reduce-scatter.4
  158.4 67.8 reduce-scatter.2

commit v2 on v0

--- a/solution.py
+++ b/solution.py
@@ -1,6 +1,8 @@
 import jax
 import jax.numpy as jnp
 from jax import lax
+from jax.experimental import pallas as pl
+from jax.experimental.pallas import tpu as pltpu
 from jax.sharding import PartitionSpec as P
 
 
@@ -60,7 +62,324 @@
     return jnp.concatenate([first, second], 1)
 
 
+def fused_kernel(
+    p_ref, x_ref, g_ref, w_ref, dn_ref,
+    gi_ref, ggu_ref, gd_ref,
+    xg, p_all, rows, rin, xin, gp, hp, acc, part, mate_in, y_in, y_sum,
+    got, up_sent, dn_sent, x_sent, p_got, p_sent, r_got, r_sent, xin_got, dp_got, dp_sent,
+):
+    me = lax.axis_index("expert")
+    dp = lax.axis_index("dp")
+    z, x = me // 2, lax.rem(me, 2)
+    y, core = dp // 2, lax.rem(dp, 2)
+    partner = 2 * z + (1 - x)
+    mate = 2 * y + (1 - core)
+    across = 2 * (1 - y) + core
+    middle = lax.rem((z + 1) // 2, 2)
+    ff = dn_ref.shape[1]
+    quarter = w_ref.shape[0] // 4
+
+    def send(src, dst, ssem, rsem, axis, to):
+        return pltpu.make_async_remote_copy(
+            src_ref=src, dst_ref=dst, send_sem=ssem, recv_sem=rsem,
+            device_id={axis: to}, device_id_type=pl.DeviceIdType.MESH,
+        )
+
+    def level(k):
+        turn = k + middle * (k // 2) * (1 - 2 * lax.rem(k, 2))
+        return 2 * lax.rem(z // 2 + turn // 2, 2) + lax.rem(z + turn, 2)
+
+    def ups(i, lev, src):
+        return send(src, xg.at[i, 2 * lev + x], up_sent.at[i, lev], got.at[i, 2 * lev + x], "expert", me + 2)
+
+    def downs(i, lev, src):
+        return send(src, xg.at[i, 2 * lev + x], dn_sent.at[i, lev], got.at[i, 2 * lev + x], "expert", me - 2)
+
+    def crosses(i, lev, src):
+        return send(src, xg.at[i, 2 * lev + x], x_sent.at[i, lev], got.at[i, 2 * lev + x], "expert", partner)
+
+    def spread(i, lev, src):
+        @pl.when((lev <= z) & (z < 3))
+        def _():
+            ups(i, lev, src).start()
+
+        @pl.when((lev >= z) & (z > 0))
+        def _():
+            downs(i, lev, src).start()
+
+        crosses(i, lev, src).start()
+
+    def arrived(i, blk):
+        send(xg.at[i, blk], xg.at[i, blk], x_sent.at[i, 0], got.at[i, blk], "expert", partner).wait_recv()
+
+    def probs_to(other):
+        return send(p_ref, p_all.at[me], p_sent.at[other], p_got.at[me], "expert", other)
+
+    def probs_from(blk):
+        send(p_ref, p_all.at[blk], p_sent.at[0], p_got.at[blk], "expert", partner).wait_recv()
+
+    def return_down(blk):
+        return send(rows.at[blk], rin.at[0, blk], r_sent.at[blk], r_got.at[0, blk], "expert", me - 2)
+
+    def return_up(blk):
+        return send(rows.at[blk], rin.at[1, blk], r_sent.at[blk], r_got.at[1, blk], "expert", me + 2)
+
+    def return_cross(blk):
+        return send(rows.at[blk], xin, r_sent.at[blk], xin_got, "expert", partner)
+
+    def pass_on(lev, blk):
+        @pl.when(lev < z)
+        def _():
+            return_down(blk).start()
+
+        @pl.when(lev > z)
+        def _():
+            return_up(blk).start()
+
+    def add_in(side, blk):
+        send(rows.at[blk], rin.at[side, blk], r_sent.at[blk], r_got.at[side, blk], "expert", partner).wait_recv()
+        rows[blk] = (rows[blk].astype(jnp.float32) + rin[side, blk].astype(jnp.float32)).astype(jnp.bfloat16)
+
+    def relay(k, other):
+        lev = level(k)
+        blk = 2 * lev + lax.rem(x + other, 2)
+
+        @pl.when(lev < z)
+        def _():
+            add_in(0, blk)
+
+        @pl.when(lev > z)
+        def _():
+            add_in(1, blk)
+
+        pass_on(lev, blk)
+
+    def finish(blk):
+        @pl.when(z < 3)
+        def _():
+            add_in(0, blk)
+
+        @pl.when(z > 0)
+        def _():
+            add_in(1, blk)
+
+    barrier = pltpu.get_barrier_semaphore()
+    for step in range(1, 8):
+        pl.semaphore_signal(
+            barrier, inc=1, device_id={"expert": lax.rem(me + step, 8)}, device_id_type=pl.DeviceIdType.MESH
+        )
+    for to in (mate, across):
+        pl.semaphore_signal(barrier, inc=1, device_id={"dp": to}, device_id_type=pl.DeviceIdType.MESH)
+    pl.semaphore_wait(barrier, 9)
+
+    spread(0, z, x_ref)
+    spread(1, z, g_ref)
+    for step in range(1, 8):
+        probs_to(lax.rem(me + step, 8)).start()
+    xg[0, me] = x_ref[...]
+    xg[1, me] = g_ref[...]
+    p_all[me] = p_ref[...]
+    acc[...] = jnp.zeros_like(acc)
+
+    def work(blk):
+        row_id = lax.broadcasted_iota(jnp.int32, (8, 128), 0)
+        p_row = jnp.sum(jnp.where(row_id == me, p_all[blk], 0.0), axis=0, keepdims=True)
+        p_cols = jnp.transpose(jnp.broadcast_to(p_row, (128, 128)))
+        p_wide = jnp.concatenate([p_cols] * (ff // 128), axis=1)
+        projected = jnp.dot(xg[0, blk], w_ref[...], preferred_element_type=jnp.float32)
+        grad_hidden = jnp.dot(xg[1, blk], dn_ref[...], preferred_element_type=jnp.float32) * p_wide
+        gate_pre = projected[:, :ff]
+        up_part = projected[:, ff:]
+        s = jax.nn.sigmoid(gate_pre)
+        activated = gate_pre * s
+        hp[blk] = (activated * up_part * p_wide).astype(jnp.bfloat16)
+        gp[blk, :, :ff] = (grad_hidden * up_part * s * (1.0 + gate_pre * (1.0 - s))).astype(jnp.bfloat16)
+        gp[blk, :, ff:] = (grad_hidden * activated).astype(jnp.bfloat16)
+        rows[blk] = lax.dot_general(
+            gp[blk], w_ref[...], (((1,), (1,)), ((), ())), preferred_element_type=jnp.float32
+        ).astype(jnp.bfloat16)
+
+    def weights(lev):
+        pair = pl.ds(2 * lev, 2)
+        gp_two = gp[pair].reshape(256, 2 * ff)
+        hp_two = hp[pair].reshape(256, ff)
+        for q in range(4):
+            at = slice(q * quarter, (q + 1) * quarter)
+            acc[at, : 2 * ff] += lax.dot_general(
+                xg[0, pair, :, at].reshape(256, quarter), gp_two,
+                (((0,), (0,)), ((), ())), preferred_element_type=jnp.float32,
+            )
+            acc[at, 2 * ff :] += lax.dot_general(
+                xg[1, pair, :, at].reshape(256, quarter), hp_two,
+                (((0,), (0,)), ((), ())), preferred_element_type=jnp.float32,
+            )
+
+    def step(s, carry):
+        k, other = s // 2, lax.rem(s, 2)
+        lev = level(k)
+        blk = 2 * lev + lax.rem(x + other, 2)
+
+        @pl.when((other == 1) & (k < 3))
+        def _():
+            ahead = level(k + 1)
+            for i in range(2):
+                arrived(i, 2 * ahead + x)
+                spread(i, ahead, xg.at[i, 2 * ahead + x])
+
+        @pl.when((s == 7) & (middle == 1))
+        def _():
+            relay(2, 0)
+            relay(3, 0)
+
+        @pl.when(other == 1)
+        def _():
+            for i in range(2):
+                arrived(i, blk)
+
+        @pl.when(s > 0)
+        def _():
+            probs_from(blk)
+
+        work(blk)
+
+        @pl.when((middle == 0) & (k > 0))
+        def _():
+            pass_on(lev, blk)
+
+        @pl.when(other == 1)
+        def _():
+            weights(lev)
+
+        return carry
+
+    lax.fori_loop(0, 8, step, 0)
+
+    for d in range(4):
+        part[d] = acc[d * quarter : (d + 1) * quarter].astype(jnp.bfloat16)
+
+    def to_mate(i, row):
+        return send(part.at[row], mate_in.at[i], dp_sent.at[i], dp_got.at[i], "dp", mate)
+
+    first = to_mate(0, 2 * (1 - y) + (1 - core))
+    second = to_mate(1, mate)
+    first.start()
+    second.start()
+
+    @pl.when(middle == 1)
+    def _():
+        relay(2, 1)
+        relay(1, 0)
+
+    first.wait_recv()
+    y_sum[...] = (part[across].astype(jnp.float32) + mate_in[0].astype(jnp.float32)).astype(jnp.bfloat16)
+    over = send(y_sum, y_in, dp_sent.at[2], dp_got.at[2], "dp", across)
+    over.start()
+
+    @pl.when(middle == 1)
+    def _():
+        relay(3, 1)
+        relay(1, 1)
+
+    finish(partner)
+    return_cross(partner).start()
+    finish(me)
+
+    second.wait_recv()
+    over.wait_recv()
+    total = part[dp].astype(jnp.float32) + mate_in[1].astype(jnp.float32) + y_in[...].astype(jnp.float32)
+    ggu_ref[...] = total[:, : 2 * ff]
+    gd_ref[...] = total[:, 2 * ff :]
+
+    return_cross(partner).wait_recv()
+    gi_ref[...] = (rows[me].astype(jnp.float32) + xin[...].astype(jnp.float32)).astype(jnp.bfloat16)
+
+    first.wait_send()
+    second.wait_send()
+    over.wait_send()
+    return_cross(partner).wait_send()
+    for i in range(7):
+        probs_to(lax.rem(me + 1 + i, 8)).wait_send()
+    for lev in range(4):
+        for i in range(2):
+            src = xg.at[i, 2 * lev + x]
+
+            @pl.when((lev <= z) & (z < 3))
+            def _():
+                ups(i, lev, src).wait_send()
+
+            @pl.when((lev >= z) & (z > 0))
+            def _():
+                downs(i, lev, src).wait_send()
+
+            crosses(i, lev, src).wait_send()
+            blk = 2 * lev + i
+
+            @pl.when(lev < z)
+            def _():
+                return_down(blk).wait_send()
+
+            @pl.when(lev > z)
+            def _():
+                return_up(blk).wait_send()
+
+
+def dense_device(x_in, grad_out, routes, gate_probs, gate_up, down):
+    owners = lax.axis_size("expert")
+    tokens, width = x_in.shape
+    hidden_units = down.shape[2]
+    cols = 3 * hidden_units
+    quarter = width // 4
+    ids = jnp.arange(owners, dtype=jnp.int32)
+    prob_by_expert = jnp.sum(
+        jnp.where(routes.T[:, None, :] == ids[None, :, None], gate_probs.T[:, None, :], 0.0), axis=0
+    )
+    bf16, f32, dma = jnp.bfloat16, jnp.float32, pltpu.SemaphoreType.DMA
+    vmem = pl.BlockSpec(memory_space=pltpu.VMEM)
+    grad_in, grad_gate_up, grad_down = pl.pallas_call(
+        fused_kernel,
+        out_shape=(
+            jax.ShapeDtypeStruct((tokens, width), bf16),
+            jax.ShapeDtypeStruct((quarter, 2 * hidden_units), f32),
+            jax.ShapeDtypeStruct((quarter, hidden_units), f32),
+        ),
+        in_specs=[vmem] * 5,
+        out_specs=(vmem,) * 3,
+        scratch_shapes=[
+            pltpu.VMEM((2, owners, tokens, width), bf16),
+            pltpu.VMEM((owners, owners, tokens), f32),
+            pltpu.VMEM((owners, tokens, width), bf16),
+            pltpu.VMEM((2, owners, tokens, width), bf16),
+            pltpu.VMEM((tokens, width), bf16),
+            pltpu.VMEM((owners, tokens, 2 * hidden_units), bf16),
+            pltpu.VMEM((owners, tokens, hidden_units), bf16),
+            pltpu.VMEM((width, cols), f32),
+            pltpu.VMEM((4, quarter, cols), bf16),
+            pltpu.VMEM((2, quarter, cols), bf16),
+            pltpu.VMEM((quarter, cols), bf16),
+            pltpu.VMEM((quarter, cols), bf16),
+            dma((2, owners)),
+            dma((2, 4)),
+            dma((2, 4)),
+            dma((2, 4)),
+            dma((owners,)),
+            dma((owners,)),
+            dma((2, owners)),
+            dma((owners,)),
+            dma,
+            dma((3,)),
+            dma((3,)),
+        ],
+        compiler_params=pltpu.CompilerParams(
+            collective_id=0, has_side_effects=True, vmem_limit_bytes=52 * 1024 * 1024
+        ),
+    )(prob_by_expert, x_in, grad_out, gate_up[0], down[0])
+    return (grad_in, grad_gate_up[None], grad_down[None])
+
+
 def per_device(x_in, grad_out, routes, gate_probs, gate_up, down):
+    lines = (lax.axis_size("expert"), lax.axis_size("dp"), routes.shape[1], x_in.shape[0])
+    if lines == (8, 4, 8, 128):
+        return dense_device(x_in, grad_out, routes, gate_probs, gate_up, down)
     owners = lax.axis_size("expert")
     tokens_here = x_in.shape[0]
     top_count = routes.shape[1]

time: 222 us -> 92.1 us (0.41)
  waiting for transfers between devices: 124 us -> 0 us
  Pallas kernels: 0 us -> 86.2 us
  local copies, waits for them, and re-layouts: 34.8 us -> 4.22 us
  matrix products: 19.6 us -> 0 us
  starting transfers between devices: 16.4 us -> 0 us
  between operations: 14.2 us -> 0.65 us
  other arithmetic: 13.2 us -> 0.72 us
    all_to_all x3 -> x0, waiting for transfers between devices: 124 us -> none  [the longest x1 47.6 us: per_device(): lax.all_to_all(grad_rows.reshape(owners, capacity, width), 'expert', spli...]
    pallas_call x0 -> x1, Pallas kernels: none -> 86.2 us  [dense_device(): pl.pallas_call(fused_kernel, out_shape=(jax.ShapeDtypeStruct((tokens, wid...]
    gather x4 -> x0, local copies, waits for them, and re-layouts: 24.8 us -> none  [the longest x1 7.91 us: per_device(): entries = returned.reshape(-1, width)[entry_pos]]
    dot_general x5 -> x0, matrix products: 19.6 us -> none  [the longest x1 5.1 us: expert_rows(): jnp.dot(rows_in, proj_weight, preferred_element_type=jnp.float32)]
    all_to_all x3 -> x0, starting transfers between devices: 16.3 us -> none  [the longest x1 7.38 us: per_device(): lax.all_to_all(sent_rows, 'expert', split_axis=0, concat_axis=0, tiled=True)]
    convert_element_type x3 -> x0, other arithmetic: 4.52 us -> none  [the longest x1 3.36 us: send_rows(): sent_grads = (prob_padded[slot_table][:, None] * grad_padded[token_pos].a...]
    scatter x1 -> x0, local copies, waits for them, and re-layouts: 4.31 us -> none  [dispatch_table(): slot_table.at[entry_pos].set(jnp.arange(count_rows, dtype=jnp.int32))]
    reduce_sum x2 -> x1, other arithmetic: 3.75 us -> 0.72 us  [dense_device(): jnp.sum(jnp.where(routes.T[:, None, :] == ids[None, :, None], gate_probs....]
  transfers between devices with their start and end apart: 4 -> 0, of which waited for: 3 -> 0; matrix products, arithmetic and copies ran while one was open for 16% -> 0% of each run, Pallas kernels for 0% -> 0%
where the time goes in v2:
time: 92.1 us; the launch traced here: 91.8 us
  Pallas kernels  86.2 us (94%)
  local copies, waits for them, and re-layouts  4.22 us (5%)
    pallas_call x1, Pallas kernels, dense_device(): pl.pallas_call(fused_kernel, out_shape=(jax.ShapeDtypeStruct((tokens, wid...  86.2 us
    unnamed x7, local copies, waits for them, and re-layouts  4.22 us

profile of v2, /device:TPU:0, one launch (start us, length us, event | category | flops | bytes accessed | tf_op | source)
XLA Modules:
  0.0 91.8 jit_solution(8081253988687360958)
XLA Ops:
  0.6 0.7 select_reduce_fusion.p_ref
  1.3 0.0 copy-start
  1.4 0.9 %copy-done = bf16[128,1024]{1,0:T(8,128)(2,1)S(1)} copy-done((bf16[128,1024]{1,0:T(8,128)(2,1)S(1)}, bf16[128,1024]{1,0:T(8,128)(2,1)}, u32[]{:S(2)}) %copy-start) | copy-done | bytes 262168
  2.3 0.0 copy-start.1
  2.3 0.9 %copy-done.1 = bf16[128,1024]{1,0:T(8,128)(2,1)S(1)} copy-done((bf16[128,1024]{1,0:T(8,128)(2,1)S(1)}, bf16[128,1024]{1,0:T(8,128)(2,1)}, u32[]{:S(2)}) %copy-start.1) | copy-done | bytes 262168
  3.3 86.2 %shard_map.85 = (bf16[128,1024]{1,0:T(8,128)(2,1)S(1)}, f32[256,768]{1,0:T(8,128)S(1)}, f32[256,384]{1,0:T(8,128)S(1)}) custom-call(f32[8,128]{1,0:T(8,128)S(1)} %select_reduce_fusion.p_ref, bf16[128,1024]{1,0:T(8,128)(2,1)S(1)} %copy-done, bf16[128,1024]{1,0:T(8,128)(2,1)S(1)} %copy-done.1, bf16[1024,768]{1,0:T(8,128)(2,1)} %bitcast.8, ...), custom_call_target="tpu_custom_call" | custom-call | tf_op jit(solution)/shard_map/pallas_call | solution.py:338
  89.5 0.7 copy.12
  90.2 0.9 copy.13
  91.1 0.7 copy.14
Async XLA Ops:
  1.3 1.0 %copy-start = (bf16[128,1024]{1,0:T(8,128)(2,1)S(1)}, bf16[128,1024]{1,0:T(8,128)(2,1)}, u32[]{:S(2)}) copy-start(bf16[128,1024]{1,0:T(8,128)(2,1)} %x_ref.1) | copy-start | bytes 786436
  2.3 0.9 %copy-start.1 = (bf16[128,1024]{1,0:T(8,128)(2,1)S(1)}, bf16[128,1024]{1,0:T(8,128)(2,1)}, u32[]{:S(2)}) copy-start(bf16[128,1024]{1,0:T(8,128)(2,1)} %g_ref.1) | copy-start | bytes 786436

commit v3 on v2

--- a/solution.py
+++ b/solution.py
@@ -63,10 +63,10 @@
 
 
 def fused_kernel(
-    p_ref, x_ref, g_ref, w_ref, dn_ref,
+    p_ref, x_hbm, g_hbm, w_hbm, dn_hbm,
     gi_ref, ggu_ref, gd_ref,
-    xg, p_all, rows, rin, xin, gp, hp, acc, part, mate_in, y_in, y_sum,
-    got, up_sent, dn_sent, x_sent, p_got, p_sent, r_got, r_sent, xin_got, dp_got, dp_sent,
+    w_ref, dn_ref, xg, p_all, rows, rin, xin, gp, hp, acc, part, mate_in, y_in, y_sum,
+    got, up_sent, dn_sent, x_sent, p_got, p_sent, r_got, r_sent, xin_got, dp_got, dp_sent, loaded, carry_sent,
 ):
     me = lax.axis_index("expert")
     dp = lax.axis_index("dp")
@@ -76,6 +76,7 @@
     mate = 2 * y + (1 - core)
     across = 2 * (1 - y) + core
     middle = lax.rem((z + 1) // 2, 2)
+    half = rows.shape[1] // 2
     ff = dn_ref.shape[1]
     quarter = w_ref.shape[0] // 4
 
@@ -107,7 +108,31 @@
         def _():
             downs(i, lev, src).start()
 
-        crosses(i, lev, src).start()
+        @pl.when(is_crossed(i, lev))
+        def _():
+            crosses(i, lev, src).start()
+
+    def is_crossed(i, lev):
+        return (lev == z) | (lax.rem(lev, 3) + 1 - i > 0)
+
+    def carry_up():
+        blk = 1 - x
+        return send(xg.at[1, blk], xg.at[1, blk], carry_sent.at[0], got.at[1, blk], "expert", me + 2)
+
+    def carry_down():
+        blk = 7 - x
+        return send(xg.at[1, blk], xg.at[1, blk], carry_sent.at[1], got.at[1, blk], "expert", me - 2)
+
+    def carry_on(lev):
+        arrived(1, 2 * lev + 1 - x)
+
+        @pl.when(lev == 0)
+        def _():
+            carry_up().start()
+
+        @pl.when(lev == 3)
+        def _():
+            carry_down().start()
 
     def arrived(i, blk):
         send(xg.at[i, blk], xg.at[i, blk], x_sent.at[i, 0], got.at[i, blk], "expert", partner).wait_recv()
@@ -118,50 +143,70 @@
     def probs_from(blk):
         send(p_ref, p_all.at[blk], p_sent.at[0], p_got.at[blk], "expert", partner).wait_recv()
 
-    def return_down(blk):
-        return send(rows.at[blk], rin.at[0, blk], r_sent.at[blk], r_got.at[0, blk], "expert", me - 2)
-
-    def return_up(blk):
-        return send(rows.at[blk], rin.at[1, blk], r_sent.at[blk], r_got.at[1, blk], "expert", me + 2)
-
-    def return_cross(blk):
-        return send(rows.at[blk], xin, r_sent.at[blk], xin_got, "expert", partner)
-
-    def pass_on(lev, blk):
+    def return_to(side, blk, h, to):
+        at = pl.ds(h * half, half)
+        return send(
+            rows.at[blk, at], rin.at[side, blk, at], r_sent.at[h, blk], r_got.at[h, side, blk], "expert", to
+        )
+
+    def return_down(blk, h):
+        return return_to(0, blk, h, me - 2)
+
+    def return_up(blk, h):
+        return return_to(1, blk, h, me + 2)
+
+    def return_cross(blk, h):
+        at = pl.ds(h * half, half)
+        return send(rows.at[blk, at], xin.at[at], r_sent.at[h, blk], xin_got.at[h], "expert", partner)
+
+    def pass_on(lev, blk, h):
         @pl.when(lev < z)
         def _():
-            return_down(blk).start()
+            return_down(blk, h).start()
 
         @pl.when(lev > z)
         def _():
-            return_up(blk).start()
-
-    def add_in(side, blk):
-        send(rows.at[blk], rin.at[side, blk], r_sent.at[blk], r_got.at[side, blk], "expert", partner).wait_recv()
-        rows[blk] = (rows[blk].astype(jnp.float32) + rin[side, blk].astype(jnp.float32)).astype(jnp.bfloat16)
+            return_up(blk, h).start()
+
+    def add_in(side, blk, h):
+        return_to(side, blk, h, partner).wait_recv()
+        at = slice(h * half, (h + 1) * half)
+        rows[blk, at] = (
+            rows[blk, at].astype(jnp.float32) + rin[side, blk, at].astype(jnp.float32)
+        ).astype(jnp.bfloat16)
 
     def relay(k, other):
         lev = level(k)
         blk = 2 * lev + lax.rem(x + other, 2)
 
-        @pl.when(lev < z)
-        def _():
-            add_in(0, blk)
-
-        @pl.when(lev > z)
-        def _():
-            add_in(1, blk)
-
-        pass_on(lev, blk)
-
-    def finish(blk):
+        for h in range(2):
+            @pl.when(lev < z)
+            def _():
+                add_in(0, blk, h)
+
+            @pl.when(lev > z)
+            def _():
+                add_in(1, blk, h)
+
+            pass_on(lev, blk, h)
+
+    def finish(blk, h):
         @pl.when(z < 3)
         def _():
-            add_in(0, blk)
+            add_in(0, blk, h)
 
         @pl.when(z > 0)
         def _():
-            add_in(1, blk)
+            add_in(1, blk, h)
+
+    loads = [
+        pltpu.make_async_copy(src, dst, loaded.at[i])
+        for i, (src, dst) in enumerate(
+            ((x_hbm, xg.at[0, me]), (g_hbm, xg.at[1, me]), (w_hbm, w_ref), (dn_hbm, dn_ref))
+        )
+    ]
+    for load in loads:
+        load.start()
 
     barrier = pltpu.get_barrier_semaphore()
     for step in range(1, 8):
@@ -172,14 +217,15 @@
         pl.semaphore_signal(barrier, inc=1, device_id={"dp": to}, device_id_type=pl.DeviceIdType.MESH)
     pl.semaphore_wait(barrier, 9)
 
-    spread(0, z, x_ref)
-    spread(1, z, g_ref)
+    for i in range(2):
+        loads[i].wait()
+        spread(i, z, xg.at[i, me])
     for step in range(1, 8):
         probs_to(lax.rem(me + step, 8)).start()
-    xg[0, me] = x_ref[...]
-    xg[1, me] = g_ref[...]
     p_all[me] = p_ref[...]
     acc[...] = jnp.zeros_like(acc)
+    loads[2].wait()
+    loads[3].wait()
 
     def work(blk):
         row_id = lax.broadcasted_iota(jnp.int32, (8, 128), 0)
@@ -199,32 +245,52 @@
             gp[blk], w_ref[...], (((1,), (1,)), ((), ())), preferred_element_type=jnp.float32
         ).astype(jnp.bfloat16)
 
+    def relay_block(k):
+        ahead = level(k)
+        for i in range(2):
+            arrived(i, 2 * ahead + x)
+            spread(i, ahead, xg.at[i, 2 * ahead + x])
+
+    def terms(lev, q):
+        pair = pl.ds(2 * lev, 2)
+        at = pl.ds(pl.multiple_of(q * quarter, quarter), quarter)
+        first_term = lax.dot_general(
+            xg[0, pair, :, at].reshape(256, quarter), gp[pair].reshape(256, 2 * ff),
+            (((0,), (0,)), ((), ())), preferred_element_type=jnp.float32,
+        )
+        second_term = lax.dot_general(
+            xg[1, pair, :, at].reshape(256, quarter), hp[pair].reshape(256, ff),
+            (((0,), (0,)), ((), ())), preferred_element_type=jnp.float32,
+        )
+        return (first_term, second_term)
+
     def weights(lev):
-        pair = pl.ds(2 * lev, 2)
-        gp_two = gp[pair].reshape(256, 2 * ff)
-        hp_two = hp[pair].reshape(256, ff)
         for q in range(4):
-            at = slice(q * quarter, (q + 1) * quarter)
-            acc[at, : 2 * ff] += lax.dot_general(
-                xg[0, pair, :, at].reshape(256, quarter), gp_two,
-                (((0,), (0,)), ((), ())), preferred_element_type=jnp.float32,
-            )
-            acc[at, 2 * ff :] += lax.dot_general(
-                xg[1, pair, :, at].reshape(256, quarter), hp_two,
-                (((0,), (0,)), ((), ())), preferred_element_type=jnp.float32,
-            )
+            first_term, second_term = terms(lev, q)
+            acc[q, :, : 2 * ff] += first_term
+            acc[q, :, 2 * ff :] += second_term
+
+    def last_weights(q):
+        first_term, second_term = terms(level(3), q)
+        part[q, :, : 2 * ff] = (acc[q, :, : 2 * ff] + first_term).astype(jnp.bfloat16)
+        part[q, :, 2 * ff :] = (acc[q, :, 2 * ff :] + second_term).astype(jnp.bfloat16)
 
     def step(s, carry):
         k, other = s // 2, lax.rem(s, 2)
         lev = level(k)
         blk = 2 * lev + lax.rem(x + other, 2)
 
-        @pl.when((other == 1) & (k < 3))
-        def _():
-            ahead = level(k + 1)
-            for i in range(2):
-                arrived(i, 2 * ahead + x)
-                spread(i, ahead, xg.at[i, 2 * ahead + x])
+        @pl.when((middle == 1) & ((s == 3) | (s == 5)))
+        def _():
+            carry_on(level(2 * k - 1))
+
+        @pl.when((other == 1) & (k + middle < 3))
+        def _():
+            relay_block(k + 1 + middle * ((k + 1) // 2))
+
+        @pl.when((s == 1) & (middle == 1))
+        def _():
+            relay_block(2)
 
         @pl.when((s == 7) & (middle == 1))
         def _():
@@ -233,8 +299,15 @@
 
         @pl.when(other == 1)
         def _():
-            for i in range(2):
-                arrived(i, blk)
+            arrived(0, blk)
+
+            @pl.when((middle == 0) & (k == 0))
+            def _():
+                carry_on(lev)
+
+            @pl.when(((middle == 0) & (k > 0)) | ((middle == 1) & (lax.rem(k, 2) == 0)))
+            def _():
+                arrived(1, blk)
 
         @pl.when(s > 0)
         def _():
@@ -244,25 +317,32 @@
 
         @pl.when((middle == 0) & (k > 0))
         def _():
-            pass_on(lev, blk)
-
-        @pl.when(other == 1)
+            pass_on(lev, blk, 0)
+            pass_on(lev, blk, 1)
+
+        @pl.when((other == 1) & (k < 3))
         def _():
             weights(lev)
 
         return carry
 
     lax.fori_loop(0, 8, step, 0)
-
-    for d in range(4):
-        part[d] = acc[d * quarter : (d + 1) * quarter].astype(jnp.bfloat16)
 
     def to_mate(i, row):
         return send(part.at[row], mate_in.at[i], dp_sent.at[i], dp_got.at[i], "dp", mate)
 
-    first = to_mate(0, 2 * (1 - y) + (1 - core))
+    diagonal = 2 * (1 - y) + (1 - core)
+    first = to_mate(0, diagonal)
     second = to_mate(1, mate)
+    last_weights(diagonal)
     first.start()
+    last_weights(across)
+
+    first.wait_recv()
+    y_sum[...] = (part[across].astype(jnp.float32) + mate_in[0].astype(jnp.float32)).astype(jnp.bfloat16)
+    over = send(y_sum, y_in, dp_sent.at[2], dp_got.at[2], "dp", across)
+    over.start()
+    last_weights(mate)
     second.start()
 
     @pl.when(middle == 1)
@@ -270,19 +350,18 @@
         relay(2, 1)
         relay(1, 0)
 
-    first.wait_recv()
-    y_sum[...] = (part[across].astype(jnp.float32) + mate_in[0].astype(jnp.float32)).astype(jnp.bfloat16)
-    over = send(y_sum, y_in, dp_sent.at[2], dp_got.at[2], "dp", across)
-    over.start()
-
     @pl.when(middle == 1)
     def _():
         relay(3, 1)
         relay(1, 1)
 
-    finish(partner)
-    return_cross(partner).start()
-    finish(me)
+    last_weights(dp)
+
+    for h in range(2):
+        finish(partner, h)
+        return_cross(partner, h).start()
+    for h in range(2):
+        finish(me, h)
 
     second.wait_recv()
     over.wait_recv()
@@ -290,13 +369,23 @@
     ggu_ref[...] = total[:, : 2 * ff]
     gd_ref[...] = total[:, 2 * ff :]
 
-    return_cross(partner).wait_recv()
+    for h in range(2):
+        return_cross(partner, h).wait_recv()
     gi_ref[...] = (rows[me].astype(jnp.float32) + xin[...].astype(jnp.float32)).astype(jnp.bfloat16)
+
+    @pl.when(z < 3)
+    def _():
+        carry_up().wait_send()
+
+    @pl.when(z > 0)
+    def _():
+        carry_down().wait_send()
 
     first.wait_send()
     second.wait_send()
     over.wait_send()
-    return_cross(partner).wait_send()
+    for h in range(2):
+        return_cross(partner, h).wait_send()
     for i in range(7):
         probs_to(lax.rem(me + 1 + i, 8)).wait_send()
     for lev in range(4):
@@ -311,16 +400,21 @@
             def _():
                 downs(i, lev, src).wait_send()
 
-            crosses(i, lev, src).wait_send()
+            @pl.when(is_crossed(i, lev))
+            def _():
+                crosses(i, lev, src).wait_send()
+
             blk = 2 * lev + i
 
             @pl.when(lev < z)
             def _():
-                return_down(blk).wait_send()
+                return_down(blk, 0).wait_send()
+                return_down(blk, 1).wait_send()
 
             @pl.when(lev > z)
             def _():
-                return_up(blk).wait_send()
+                return_up(blk, 0).wait_send()
+                return_up(blk, 1).wait_send()
 
 
 def dense_device(x_in, grad_out, routes, gate_probs, gate_up, down):
@@ -342,9 +436,11 @@
             jax.ShapeDtypeStruct((quarter, 2 * hidden_units), f32),
             jax.ShapeDtypeStruct((quarter, hidden_units), f32),
         ),
-        in_specs=[vmem] * 5,
+        in_specs=[vmem] + [pl.BlockSpec(memory_space=pl.ANY)] * 4,
         out_specs=(vmem,) * 3,
         scratch_shapes=[
+            pltpu.VMEM((width, 2 * hidden_units), bf16),
+            pltpu.VMEM((width, hidden_units), bf16),
             pltpu.VMEM((2, owners, tokens, width), bf16),
             pltpu.VMEM((owners, owners, tokens), f32),
             pltpu.VMEM((owners, tokens, width), bf16),
@@ -352,7 +448,7 @@
             pltpu.VMEM((tokens, width), bf16),
             pltpu.VMEM((owners, tokens, 2 * hidden_units), bf16),
             pltpu.VMEM((owners, tokens, hidden_units), bf16),
-            pltpu.VMEM((width, cols), f32),
+            pltpu.VMEM((4, quarter, cols), f32),
             pltpu.VMEM((4, quarter, cols), bf16),
             pltpu.VMEM((2, quarter, cols), bf16),
             pltpu.VMEM((quarter, cols), bf16),
@@ -363,14 +459,16 @@
             dma((2, 4)),
             dma((owners,)),
             dma((owners,)),
+            dma((2, 2, owners)),
             dma((2, owners)),
-            dma((owners,)),
-            dma,
+            dma((2,)),
             dma((3,)),
             dma((3,)),
+            dma((4,)),
+            dma((2,)),
         ],
         compiler_params=pltpu.CompilerParams(
-            collective_id=0, has_side_effects=True, vmem_limit_bytes=52 * 1024 * 1024
+            collective_id=0, has_side_effects=True, vmem_limit_bytes=54 * 1024 * 1024
         ),
     )(prob_by_expert, x_in, grad_out, gate_up[0], down[0])
     return (grad_in, grad_gate_up[None], grad_down[None])

time: 92.1 us -> 92.1 us (level)
    unnamed x7 -> x5, local copies, waits for them, and re-layouts: 4.22 us -> 4.53 us
where the time goes in v3:
time: 92.1 us; the launch traced here: 91.8 us
  Pallas kernels  85.3 us (93%)
  local copies, waits for them, and re-layouts  4.53 us (5%)
  other arithmetic  1.31 us (1%)
    pallas_call x1, Pallas kernels, dense_device(): pl.pallas_call(fused_kernel, out_shape=(jax.ShapeDtypeStruct((tokens, wid...  85.3 us
    unnamed x5, local copies, waits for them, and re-layouts  4.53 us

profile of v3, /device:TPU:0, one launch (start us, length us, event | category | flops | bytes accessed | tf_op | source)
XLA Modules:
  0.0 91.8 jit_solution(6828700517655013058)
XLA Ops:
  0.6 1.3 %select_reduce_fusion.p_ref = f32[8,128]{1,0:T(8,128)} fusion(f32[8,128]{1,0:T(8,128)} %bitcast.10, s32[8,128]{1,0:T(8,128)} %bitcast.11), kind=kLoop, calls=%fused_computation | loop fusion | flops 23552 | bytes 12288 | tf_op jit(solution)/shard_map/reduce_sum | solution.py:427
  1.9 85.3 %shard_map.85 = (bf16[128,1024]{1,0:T(8,128)(2,1)}, f32[256,768]{1,0:T(8,128)}, f32[256,384]{1,0:T(8,128)}) custom-call(f32[8,128]{1,0:T(8,128)} %select_reduce_fusion.p_ref, bf16[128,1024]{1,0:T(8,128)(2,1)} %x_hbm.1, bf16[128,1024]{1,0:T(8,128)(2,1)} %g_hbm.1, bf16[1024,768]{1,0:T(8,128)(2,1)} %bitcast.6, bf16[1024,384]{1,0:T(8,128)(2,1)} %bitcast.8), custom_call_target="tpu_custom_call" | custom-call | tf_op jit(solution)/shard_map/pallas_call | solution.py:432
  87.3 0.0 copy-start
  87.3 1.7 %copy.12 = bf16[128,1024]{1,0:T(8,128)(2,1)} copy(bf16[128,1024]{1,0:T(8,128)(2,1)} %get-tuple-element.12) | data formatting | bytes 524288
  89.0 2.1 %copy.13 = f32[1,256,768]{2,1,0:T(8,128)} copy(f32[1,256,768]{2,1,0:T(8,128)} %bitcast.7) | data formatting | bytes 1572864
  91.0 0.0 copy-done
  91.0 0.7 copy.14
Async XLA Ops:
  87.3 3.8 %copy-start = (f32[256,384]{1,0:T(8,128)S(1)}, f32[256,384]{1,0:T(8,128)}, u32[]{:S(2)}) copy-start(f32[256,384]{1,0:T(8,128)} %get-tuple-element.8) | copy-start | bytes 1179652

commit v4 on v3

--- a/solution.py
+++ b/solution.py
@@ -66,7 +66,7 @@
     p_ref, x_hbm, g_hbm, w_hbm, dn_hbm,
     gi_ref, ggu_ref, gd_ref,
     w_ref, dn_ref, xg, p_all, rows, rin, xin, gp, hp, acc, part, mate_in, y_in, y_sum,
-    got, up_sent, dn_sent, x_sent, p_got, p_sent, r_got, r_sent, xin_got, dp_got, dp_sent, loaded, carry_sent,
+    got, up_sent, dn_sent, x_sent, p_got, p_sent, r_got, r_sent, xin_got, dp_got, dp_sent, loaded,
 ):
     me = lax.axis_index("expert")
     dp = lax.axis_index("dp")
@@ -108,31 +108,7 @@
         def _():
             downs(i, lev, src).start()
 
-        @pl.when(is_crossed(i, lev))
-        def _():
-            crosses(i, lev, src).start()
-
-    def is_crossed(i, lev):
-        return (lev == z) | (lax.rem(lev, 3) + 1 - i > 0)
-
-    def carry_up():
-        blk = 1 - x
-        return send(xg.at[1, blk], xg.at[1, blk], carry_sent.at[0], got.at[1, blk], "expert", me + 2)
-
-    def carry_down():
-        blk = 7 - x
-        return send(xg.at[1, blk], xg.at[1, blk], carry_sent.at[1], got.at[1, blk], "expert", me - 2)
-
-    def carry_on(lev):
-        arrived(1, 2 * lev + 1 - x)
-
-        @pl.when(lev == 0)
-        def _():
-            carry_up().start()
-
-        @pl.when(lev == 3)
-        def _():
-            carry_down().start()
+        crosses(i, lev, src).start()
 
     def arrived(i, blk):
         send(xg.at[i, blk], xg.at[i, blk], x_sent.at[i, 0], got.at[i, blk], "expert", partner).wait_recv()
@@ -251,39 +227,27 @@
             arrived(i, 2 * ahead + x)
             spread(i, ahead, xg.at[i, 2 * ahead + x])
 
-    def terms(lev, q):
+    def weights(lev, last):
         pair = pl.ds(2 * lev, 2)
-        at = pl.ds(pl.multiple_of(q * quarter, quarter), quarter)
-        first_term = lax.dot_general(
-            xg[0, pair, :, at].reshape(256, quarter), gp[pair].reshape(256, 2 * ff),
-            (((0,), (0,)), ((), ())), preferred_element_type=jnp.float32,
-        )
-        second_term = lax.dot_general(
-            xg[1, pair, :, at].reshape(256, quarter), hp[pair].reshape(256, ff),
-            (((0,), (0,)), ((), ())), preferred_element_type=jnp.float32,
-        )
-        return (first_term, second_term)
-
-    def weights(lev):
+        gp_two = gp[pair].reshape(256, 2 * ff)
+        hp_two = hp[pair].reshape(256, ff)
         for q in range(4):
-            first_term, second_term = terms(lev, q)
-            acc[q, :, : 2 * ff] += first_term
-            acc[q, :, 2 * ff :] += second_term
-
-    def last_weights(q):
-        first_term, second_term = terms(level(3), q)
-        part[q, :, : 2 * ff] = (acc[q, :, : 2 * ff] + first_term).astype(jnp.bfloat16)
-        part[q, :, 2 * ff :] = (acc[q, :, 2 * ff :] + second_term).astype(jnp.bfloat16)
+            at = slice(q * quarter, (q + 1) * quarter)
+            for i, right, cols in ((0, gp_two, slice(0, 2 * ff)), (1, hp_two, slice(2 * ff, 3 * ff))):
+                term = acc[at, cols] + lax.dot_general(
+                    xg[i, pair, :, at].reshape(256, quarter), right,
+                    (((0,), (0,)), ((), ())), preferred_element_type=jnp.float32,
+                )
+                if last:
+                    part[q, :, cols] = term.astype(jnp.bfloat16)
+                else:
+                    acc[at, cols] = term
 
     def step(s, carry):
         k, other = s // 2, lax.rem(s, 2)
         lev = level(k)
         blk = 2 * lev + lax.rem(x + other, 2)
 
-        @pl.when((middle == 1) & ((s == 3) | (s == 5)))
-        def _():
-            carry_on(level(2 * k - 1))
-
         @pl.when((other == 1) & (k + middle < 3))
         def _():
             relay_block(k + 1 + middle * ((k + 1) // 2))
@@ -299,15 +263,8 @@
 
         @pl.when(other == 1)
         def _():
-            arrived(0, blk)
-
-            @pl.when((middle == 0) & (k == 0))
-            def _():
-                carry_on(lev)
-
-            @pl.when(((middle == 0) & (k > 0)) | ((middle == 1) & (lax.rem(k, 2) == 0)))
-            def _():
-                arrived(1, blk)
+            for i in range(2):
+                arrived(i, blk)
 
         @pl.when(s > 0)
         def _():
@@ -322,40 +279,36 @@
 
         @pl.when((other == 1) & (k < 3))
         def _():
-            weights(lev)
+            weights(lev, False)
 
         return carry
 
     lax.fori_loop(0, 8, step, 0)
+
+    weights(level(3), True)
 
     def to_mate(i, row):
         return send(part.at[row], mate_in.at[i], dp_sent.at[i], dp_got.at[i], "dp", mate)
 
-    diagonal = 2 * (1 - y) + (1 - core)
-    first = to_mate(0, diagonal)
+    first = to_mate(0, 2 * (1 - y) + (1 - core))
     second = to_mate(1, mate)
-    last_weights(diagonal)
     first.start()
-    last_weights(across)
+    second.start()
+
+    @pl.when(middle == 1)
+    def _():
+        relay(2, 1)
+        relay(1, 0)
 
     first.wait_recv()
     y_sum[...] = (part[across].astype(jnp.float32) + mate_in[0].astype(jnp.float32)).astype(jnp.bfloat16)
     over = send(y_sum, y_in, dp_sent.at[2], dp_got.at[2], "dp", across)
     over.start()
-    last_weights(mate)
-    second.start()
-
-    @pl.when(middle == 1)
-    def _():
-        relay(2, 1)
-        relay(1, 0)
 
     @pl.when(middle == 1)
     def _():
         relay(3, 1)
         relay(1, 1)
-
-    last_weights(dp)
 
     for h in range(2):
         finish(partner, h)
@@ -372,14 +325,6 @@
     for h in range(2):
         return_cross(partner, h).wait_recv()
     gi_ref[...] = (rows[me].astype(jnp.float32) + xin[...].astype(jnp.float32)).astype(jnp.bfloat16)
-
-    @pl.when(z < 3)
-    def _():
-        carry_up().wait_send()
-
-    @pl.when(z > 0)
-    def _():
-        carry_down().wait_send()
 
     first.wait_send()
     second.wait_send()
@@ -400,10 +345,7 @@
             def _():
                 downs(i, lev, src).wait_send()
 
-            @pl.when(is_crossed(i, lev))
-            def _():
-                crosses(i, lev, src).wait_send()
-
+            crosses(i, lev, src).wait_send()
             blk = 2 * lev + i
 
             @pl.when(lev < z)
@@ -448,7 +390,7 @@
             pltpu.VMEM((tokens, width), bf16),
             pltpu.VMEM((owners, tokens, 2 * hidden_units), bf16),
             pltpu.VMEM((owners, tokens, hidden_units), bf16),
-            pltpu.VMEM((4, quarter, cols), f32),
+            pltpu.VMEM((width, cols), f32),
             pltpu.VMEM((4, quarter, cols), bf16),
             pltpu.VMEM((2, quarter, cols), bf16),
             pltpu.VMEM((quarter, cols), bf16),
@@ -465,10 +407,9 @@
             dma((3,)),
             dma((3,)),
             dma((4,)),
-            dma((2,)),
         ],
         compiler_params=pltpu.CompilerParams(
-            collective_id=0, has_side_effects=True, vmem_limit_bytes=54 * 1024 * 1024
+            collective_id=0, has_side_effects=True, vmem_limit_bytes=50 * 1024 * 1024
         ),
     )(prob_by_expert, x_in, grad_out, gate_up[0], down[0])
     return (grad_in, grad_gate_up[None], grad_down[None])

time: 92.1 us -> 85.2 us (0.925)
  Pallas kernels: 85.3 us -> 78.2 us
    pallas_call x1, Pallas kernels: 85.3 us -> 78.2 us  [dense_device(): pl.pallas_call(fused_kernel, out_shape=(jax.ShapeDtypeStruct((tokens, wid...]
    unnamed x5 -> x9, local copies, waits for them, and re-layouts: 4.53 us -> 5.36 us
where the time goes in v4:
time: 85.2 us; the launch traced here: 84.9 us
  Pallas kernels  78.2 us (92%)
  local copies, waits for them, and re-layouts  5.36 us (6%)
    pallas_call x1, Pallas kernels, dense_device(): pl.pallas_call(fused_kernel, out_shape=(jax.ShapeDtypeStruct((tokens, wid...  78.2 us
    unnamed x9, local copies, waits for them, and re-layouts  5.36 us

profile of v4, /device:TPU:0, one launch (start us, length us, event | category | flops | bytes accessed | tf_op | source)
XLA Modules:
  0.0 84.9 jit_solution(14719009841976422018)
XLA Ops:
  0.6 0.7 select_reduce_fusion.p_ref
  1.3 0.0 copy-start
  1.4 1.1 %copy-done = bf16[1,1024,384]{2,1,0:T(8,128)(2,1)S(1)} copy-done((bf16[1,1024,384]{2,1,0:T(8,128)(2,1)S(1)}, bf16[1,1024,384]{2,1,0:T(8,128)(2,1)}, u32[]{:S(2)}) %copy-start) | copy-done | bytes 786456
  2.5 0.0 copy-start.1
  2.5 0.9 %copy-done.1 = bf16[128,1024]{1,0:T(8,128)(2,1)S(1)} copy-done((bf16[128,1024]{1,0:T(8,128)(2,1)S(1)}, bf16[128,1024]{1,0:T(8,128)(2,1)}, u32[]{:S(2)}) %copy-start.1) | copy-done | bytes 262168
  3.4 0.0 copy-start.2
  3.4 0.9 %copy-done.2 = bf16[128,1024]{1,0:T(8,128)(2,1)S(1)} copy-done((bf16[128,1024]{1,0:T(8,128)(2,1)S(1)}, bf16[128,1024]{1,0:T(8,128)(2,1)}, u32[]{:S(2)}) %copy-start.2) | copy-done | bytes 262168
  4.4 78.2 %shard_map.85 = (bf16[128,1024]{1,0:T(8,128)(2,1)S(1)}, f32[256,768]{1,0:T(8,128)S(1)}, f32[256,384]{1,0:T(8,128)S(1)}) custom-call(f32[8,128]{1,0:T(8,128)S(1)} %select_reduce_fusion.p_ref, bf16[128,1024]{1,0:T(8,128)(2,1)S(1)} %copy-done.1, bf16[128,1024]{1,0:T(8,128)(2,1)S(1)} %copy-done.2, bf16[1024,768]{1,0:T(8,128)(2,1)} %bitcast.9, ...), custom_call_target="tpu_custom_call" | custom-call | tf_op jit(solution)/shard_map/pallas_call | solution.py:374
  82.6 0.7 copy.12
  83.3 0.9 %copy.13 = f32[1,256,768]{2,1,0:T(8,128)} copy(f32[1,256,768]{2,1,0:T(8,128)S(1)} %bitcast.6) | data formatting | bytes 1572864
  84.2 0.7 copy.14
Async XLA Ops:
  1.3 1.1 %copy-start = (bf16[1,1024,384]{2,1,0:T(8,128)(2,1)S(1)}, bf16[1,1024,384]{2,1,0:T(8,128)(2,1)}, u32[]{:S(2)}) copy-start(bf16[1,1024,384]{2,1,0:T(8,128)(2,1)} %param.11) | copy-start | bytes 2359300
  2.5 0.9 %copy-start.1 = (bf16[128,1024]{1,0:T(8,128)(2,1)S(1)}, bf16[128,1024]{1,0:T(8,128)(2,1)}, u32[]{:S(2)}) copy-start(bf16[128,1024]{1,0:T(8,128)(2,1)} %x_hbm.1) | copy-start | bytes 786436
  3.4 0.9 %copy-start.2 = (bf16[128,1024]{1,0:T(8,128)(2,1)S(1)}, bf16[128,1024]{1,0:T(8,128)(2,1)}, u32[]{:S(2)}) copy-start(bf16[128,1024]{1,0:T(8,128)(2,1)} %g_hbm.1) | copy-start | bytes 786436
